TPU v7x, 32 devices: a whole 2x2x4 slice. The times are simulated.
32 devices in a mesh: ka: 8 (over y, x, core), pb: 4 (over z).
Axes of the slice: x: 2, y: 2, z: 4, core: 2. Of those that a mesh axis runs over, the one named last changes fastest.
Arguments:
- coupling: float32 [256, 16, 2, 64, 128], P('ka', 'pb'), may hold values from -6 to 6
- gauge: float32 [256, 64, 128], P('ka'), may hold values from -0.5 to 0.5
- kq_index: int32 [16, 256], P(None, 'ka'), may hold values from 0 to 255, as said below
- fine_coords: int32 [3, 16], replicated, may hold values from 0 to 31
- eig_right: float32 [16, 64, 128], P('ka'), may hold values from -0.5 to 0.5
- eig_left: float32 [16, 16, 64, 128], P('ka', 'pb'), may hold values from -0.5 to 0.5
- energy_k: float32 [16, 64], P('ka'), may hold values from -4 to 4
- energy_kq: float32 [16, 16, 64], P('ka', 'pb'), may hold values from -4 to 4
- occupied: int32 [16, 16, 64], P('ka', 'pb'), may hold values 0 or 1
- frequency: float32 [16, 2], P('pb'), may hold values from 0.02 to 0.12
Outputs:
- self_energy: float32 [16, 64], P('ka')
Inputs may be any that keep to these rules, and one draw needn't show every extreme that they name: kq_index[q, k] is the number of the coarse point k displaced by the q-th window point's offset on the periodic 8 x 8 x 4 grid; for each q it is a permutation of the coarse points. Among the offsets are (4, 0, 0) and (0, 0, 3).
All inputs are finite; a program needn't handle non-finite values. No bound on the sum of `occupied` on one device may be relied on, other than what follows from the above.
Results may differ from a plain program's by a relative error of at most 0.0001.
Values sent between devices are 32-bit elements; how exact they have to be, the bound alone decides.
A program may use at most 128 MiB of HBM per device.

v0:
```python
import math

import jax
import jax.numpy as jnp
from jax import lax
from jax.sharding import PartitionSpec as P

GX = 8
GY = 8
GZ = 4
FG = 32
NK = 256


PRECISE = lax.Precision.HIGHEST
BROADEN = 0.1
THERMAL = 0.05


def product(left_matrix, right_matrix):
    return jnp.dot(left_matrix, right_matrix, precision=PRECISE, preferred_element_type=jnp.float32)


def mult(pattern, first, second):
    return jnp.einsum(pattern, first, second, precision=PRECISE)


def phase_tables(fine_coords):
    points = jnp.arange(NK, dtype=jnp.int32)
    along_first = points // (GY * GZ)
    along_second = points // GZ % GY
    along_third = points % GZ
    cell_first = along_first - GX // 2
    cell_second = along_second - GY // 2
    cell_third = along_third - GZ // 2
    coarse_index = (
        cell_first[:, None] * along_first[None, :] * (GY * GZ)
        + cell_second[:, None] * along_second[None, :] * (GX * GZ)
        + cell_third[:, None] * along_third[None, :] * (GX * GY)
    ) % NK
    coarse_angles = coarse_index.astype(jnp.float32) * (2.0 * math.pi / NK)
    fine_index = (
        fine_coords[0][:, None] * cell_first[None, :]
        + fine_coords[1][:, None] * cell_second[None, :]
        + fine_coords[2][:, None] * cell_third[None, :]
    ) % FG
    fine_angles = fine_index.astype(jnp.float32) * (2.0 * math.pi / FG)
    return (
        jnp.cos(coarse_angles) / NK,
        -jnp.sin(coarse_angles) / NK,
        jnp.cos(fine_angles),
        jnp.sin(fine_angles),
    )


def right_block(matrix):
    orbitals = matrix.shape[-2]
    real_part = matrix[..., :orbitals]
    imag_part = matrix[..., orbitals:]
    upper_half = jnp.concatenate([real_part, imag_part], -1)
    lower_half = jnp.concatenate([-imag_part, real_part], -1)
    return jnp.concatenate([upper_half, lower_half], -2)


def sectioned(cols_real, cols_imag, tables):
    coarse_real, coarse_imag, fine_cos, fine_sin = tables
    space_real = product(coarse_real, cols_real) - product(coarse_imag, cols_imag)
    space_imag = product(coarse_real, cols_imag) + product(coarse_imag, cols_real)
    fine_real_part = product(fine_cos, space_real) - product(fine_sin, space_imag)
    fine_imag_part = product(fine_cos, space_imag) + product(fine_sin, space_real)
    return (fine_real_part, fine_imag_part)


def self_terms(strength, energy_k, energy_kq, occupied, frequency):
    phonon = frequency[None, :, :, None, None]
    bose_factor = 1.0 / (jnp.exp(phonon / THERMAL) - 1.0)
    filled = occupied.astype(jnp.float32)[:, :, None, :, None]
    energy_gap = energy_k[:, None, None, None, :] - energy_kq[:, :, None, :, None]
    shifted_up = energy_gap + phonon
    shifted_down = energy_gap - phonon
    kernel = (bose_factor + filled) * shifted_up / (shifted_up * shifted_up + BROADEN * BROADEN)
    kernel = kernel + (bose_factor + 1.0 - filled) * shifted_down / (
        shifted_down * shifted_down + BROADEN * BROADEN
    )
    return jnp.sum(strength / (2.0 * phonon) * kernel, axis=(1, 2, 3))


def select_rows(wanted, block_rows):
    positions = jnp.arange(block_rows.shape[0], dtype=jnp.int32)
    onehot = (wanted[:, None] == positions[None, :]).astype(jnp.float32)
    return product(onehot, block_rows.reshape(block_rows.shape[0], -1))


def shards(
    coupling,
    gauge,
    kq_index,
    fine_coords,
    eig_right,
    eig_left,
    energy_k,
    energy_kq,
    occupied,
    frequency,
):
    coarse_rows = coupling.shape[0]
    qpoint_rows = coupling.shape[1]
    branches = coupling.shape[2]
    orbitals = coupling.shape[3]
    pb_count = lax.axis_size("pb")
    tables = phase_tables(fine_coords)
    fine_total = fine_coords.shape[1]
    own_rows = lax.dynamic_slice_in_dim(
        kq_index, lax.axis_index("pb") * qpoint_rows, qpoint_rows, 0
    )
    wanted = own_rows.T.reshape(-1)
    picked = select_rows(wanted, lax.all_gather(gauge, "ka", axis=0, tiled=True))
    left_gauge = picked.reshape(coarse_rows, qpoint_rows, orbitals, 2 * orbitals)
    right_gauge = mult("kqbjc,kcd->kqbjd", coupling, right_block(gauge))
    right_real = right_gauge[..., :orbitals]
    right_imag = right_gauge[..., orbitals:]
    left_real = left_gauge[..., :orbitals]
    left_imag = left_gauge[..., orbitals:]
    wannier_real = mult("kqjm,kqbjn->kqbmn", left_real, right_real) + mult(
        "kqjm,kqbjn->kqbmn", left_imag, right_imag
    )
    wannier_imag = mult("kqjm,kqbjn->kqbmn", left_real, right_imag) - mult(
        "kqjm,kqbjn->kqbmn", left_imag, right_real
    )
    pair_major = jnp.stack([wannier_real, wannier_imag], 1).reshape(
        coarse_rows, 2, qpoint_rows, branches, orbitals * orbitals
    )
    arrived_block = lax.all_to_all(pair_major, "ka", split_axis=4, concat_axis=0, tiled=True)
    columns = arrived_block.reshape(arrived_block.shape[0], 2, -1)
    fine_real_part, fine_imag_part = sectioned(columns[:, 0], columns[:, 1], tables)
    fine_cols = jnp.stack([fine_real_part, fine_imag_part], 1).reshape(
        (fine_total, 2) + arrived_block.shape[2:]
    )
    fine_coupling = lax.all_to_all(fine_cols, "ka", split_axis=0, concat_axis=4, tiled=True)
    fine_rows = fine_coupling.shape[0]
    arrived_parts = fine_coupling.reshape(fine_rows, 2, qpoint_rows, branches, orbitals, orbitals)
    coupled_real = arrived_parts[:, 0]
    coupled_imag = arrived_parts[:, 1]
    vector_real = eig_right[..., :orbitals]
    vector_imag = eig_right[..., orbitals:]
    half_real = mult("fqbjc,fcd->fqbjd", coupled_real, vector_real) - mult(
        "fqbjc,fcd->fqbjd", coupled_imag, vector_imag
    )
    half_imag = mult("fqbjc,fcd->fqbjd", coupled_real, vector_imag) + mult(
        "fqbjc,fcd->fqbjd", coupled_imag, vector_real
    )
    outer_real = eig_left[..., :orbitals]
    outer_imag = eig_left[..., orbitals:]
    bloch_real = mult("fqjm,fqbjn->fqbmn", outer_real, half_real) + mult(
        "fqjm,fqbjn->fqbmn", outer_imag, half_imag
    )
    bloch_imag = mult("fqjm,fqbjn->fqbmn", outer_real, half_imag) - mult(
        "fqjm,fqbjn->fqbmn", outer_imag, half_real
    )
    strength = bloch_real * bloch_real + bloch_imag * bloch_imag
    contrib = self_terms(strength, energy_k, energy_kq, occupied, frequency)
    summed = lax.psum(contrib, "pb")
    return summed / (qpoint_rows * pb_count * orbitals)


def solution(mesh):
    in_specs = (
        P("ka", "pb", None, None, None),
        P("ka", None, None),
        P(None, "ka"),
        P(),
        P("ka", None, None),
        P("ka", "pb", None, None),
        P("ka", None),
        P("ka", "pb", None),
        P("ka", "pb", None),
        P("pb", None),
    )
    out_specs = P("ka", None)
    return jax.shard_map(shards, mesh=mesh, in_specs=in_specs, out_specs=out_specs, check_vma=False)
```

profile of v0, /device:TPU:0, one launch (start us, length us, event | category | flops | bytes accessed | tf_op | source)
XLA Modules:
  0.0 611.8 jit_solution(7766570967013048343)
XLA Ops:
  6.5 0.7 all-gather.2.cloned.1.call-update
  7.3 2.0 slice_negate_fusion
  9.3 11.1 %convolution_bitcast_fusion = f32[32,4,2,64,128]{4,3,2,1,0:T(8,128)} fusion(f32[32,4,2,64,128]{4,3,2,1,0:T(8,128)} %param.10, f32[32,64,64]{2,1,0:T(8,128)S(1)} %get-tuple-element.10, f32[32,64,64]{2,1,0:T(8,128)S(1)} %get-tuple-element.9, f32[32,64,128]{2,1,0:T(8,128)S(1)} %copy-done.5), kind=kOutput, calls=%fused_computation.27 | convolution fusion | flops 3222274048 | bytes 18874368 | tf_op jit(solution)/shard_map/kqbjc,kcd->kqbjd/dot_general | solution.py:25
  20.5 45.9 %all-gather.2.cloned.1.call-done = f32[256,64,128]{2,1,0:T(8,128)} async-done(((f32[32,64,128]{2,1,0:T(8,128)}), f32[256,64,128]{2,1,0:T(8,128)}) %all-gather.2.cloned.1.call-update) | async-done | bytes 8388624 | tf_op jit(solution)/shard_map/all_gather | solution.py:117
  66.4 9.2 %copy.82 = f32[256,64,128]{0,2,1:T(8,128)} copy(f32[256,64,128]{2,1,0:T(8,128)} %all-gather.2.cloned.1.call-done) | data formatting | bytes 16777216 | tf_op jit(solution)/shard_map/reshape | solution.py:91
  75.6 10.3 %fusion = f32[32,4,64,128]{3,0,2,1:T(8,128)} fusion(f32[256,64,128]{0,2,1:T(8,128)} %copy.82, s32[32,4]{0,1:T(4,128)S(1)} %dynamic-slice_bitcast_fusion), kind=kOutput, calls=%fused_computation.1 | convolution fusion | flops 3221258240 | bytes 12583424 | tf_op jit(solution)/shard_map/dot_general | solution.py:21
  85.9 5.1 slice_bitcast_fusion.2
  91.0 21.9 %fusion.4 = f32[32,4,2,64,64]{4,3,2,1,0:T(8,128)} fusion(f32[32,4,2,64,128]{4,3,2,1,0:T(8,128)S(1)} %bitcast.128, f32[32,4,64,64,1]{3,0,2,1,4:T(8,128)S(1)} %get-tuple-element.7), kind=kOutput, calls=%fused_computation.7 | convolution fusion | flops 805306368 | bytes 14680064 | tf_op jit(solution)/shard_map/kqjm,kqbjn->kqbmn/dot_general | solution.py:25
  112.9 22.1 %fusion.2 = f32[32,4,2,64,64]{4,3,2,1,0:T(8,128)} fusion(f32[32,4,2,64,128]{4,3,2,1,0:T(8,128)S(1)} %bitcast.128, f32[32,4,64,64,1]{3,0,2,1,4:T(8,128)S(1)} %get-tuple-element.8), kind=kOutput, calls=%fused_computation.5 | convolution fusion | flops 805306368 | bytes 14680064 | tf_op jit(solution)/shard_map/kqjm,kqbjn->kqbmn/dot_general | solution.py:25
  135.0 19.1 %add_bitcast_fusion = f32[32,4,2,64,64]{3,4,2,1,0:T(8,128)} fusion(f32[32,4,2,64,64]{4,3,2,1,0:T(8,128)} %fusion.4, f32[32,4,64,64,1]{3,0,2,1,4:T(8,128)S(1)} %get-tuple-element.8, f32[32,4,2,64,128]{4,3,2,1,0:T(8,128)S(1)} %bitcast.128), kind=kOutput, calls=%fused_computation.4 | convolution fusion | flops 806354944 | bytes 18874368 | tf_op jit(solution)/shard_map/kqjm,kqbjn->kqbmn/dot_general | solution.py:25
  154.0 9.0 %copy.51 = f32[32,4,2,64,64]{4,3,0,2,1:T(8,128)} copy(f32[32,4,2,64,64]{3,4,2,1,0:T(8,128)} %add_bitcast_fusion) | data formatting | bytes 8388608 | tf_op jit(solution)/shard_map/add | solution.py:124
  163.0 7.9 %stack.18 = f32[32,1,4,2,4096]{4,0,3,2,1:T(8,128)} reshape(f32[32,4,2,64,64]{4,3,0,2,1:T(8,128)} %copy.51) | data formatting | bytes 8388608 | tf_op jit(solution)/shard_map/stack | solution.py:130
  170.9 27.3 %subtract_bitcast_fusion = f32[32,4,2,64,64]{3,4,2,1,0:T(8,128)} fusion(f32[32,4,2,64,64]{4,3,2,1,0:T(8,128)} %fusion.2, f32[32,4,64,64,1]{3,0,2,1,4:T(8,128)} %copy-done.3, f32[32,4,2,64,128]{4,3,2,1,0:T(8,128)} %convolution_bitcast_fusion), kind=kOutput, calls=%fused_computation.3 | convolution fusion | flops 806354944 | bytes 18874368 | tf_op jit(solution)/shard_map/kqjm,kqbjn->kqbmn/dot_general | solution.py:25
  198.3 9.0 %copy.56 = f32[32,4,2,64,64]{4,3,0,2,1:T(8,128)} copy(f32[32,4,2,64,64]{3,4,2,1,0:T(8,128)} %subtract_bitcast_fusion) | data formatting | bytes 8388608 | tf_op jit(solution)/shard_map/sub | solution.py:127
  207.2 8.1 %stack.19 = f32[32,1,4,2,4096]{4,0,3,2,1:T(8,128)} reshape(f32[32,4,2,64,64]{4,3,0,2,1:T(8,128)} %copy.56) | data formatting | bytes 8388608 | tf_op jit(solution)/shard_map/stack | solution.py:130
  215.4 7.7 %pad_maximum_fusion = f32[32,2,4,2,4096]{4,0,3,2,1:T(8,128)} fusion(f32[32,1,4,2,4096]{4,0,3,2,1:T(8,128)} %stack.19, f32[32,1,4,2,4096]{4,0,3,2,1:T(8,128)} %stack.18), kind=kLoop, calls=%fused_computation | loop fusion | flops 2097152 | bytes 16777216 | tf_op jit(solution)/shard_map/stack | solution.py:130
  223.1 40.1 %copy.57 = f32[32,2,4,2,4096]{0,3,2,1,4:T(2,128)} copy(f32[32,2,4,2,4096]{4,0,3,2,1:T(8,128)} %pad_maximum_fusion) | data formatting | bytes 16777216 | tf_op jit(solution)/shard_map/stack | solution.py:130
  263.2 35.5 %reshape.195 = f32[8,1,262144]{2,1,0:T(1,128)} reshape(f32[4096,2,4,2,32]{4,3,2,1,0:T(2,128)} %bitcast.129) | data formatting | bytes 16777216
  298.7 5.1 all-to-all-start
  303.8 94.0 %all-to-all-done = f32[8,1,262144]{2,1,0:T(1,128)} async-done(((f32[8,1,262144]{2,1,0:T(1,128)}), f32[8,1,262144]{2,1,0:T(1,128)}, u32[]{:S(2)}, u32[]{:S(2)}) %all-to-all-start) | async-done | bytes 8388640 | tf_op jit(solution)/shard_map/all_to_all | solution.py:133
  397.8 0.5 broadcast.461
  398.4 28.6 %reduce = f32[8,262144]{1,0:T(8,128)} reduce(f32[8,1,262144]{2,1,0:T(1,128)} %all-to-all-done, f32[]{:T(128)} %broadcast.461), dimensions={1}, to_apply=%all_to_all.22.reduce_sub_computation | reduce | bytes 16777220 | tf_op jit(solution)/shard_map/all_to_all | solution.py:133
  427.0 55.0 %reshape.196 = f32[4096,2,4,2,32]{4,3,2,1,0:T(2,128)} reshape(f32[8,262144]{1,0:T(8,128)} %reduce) | data formatting | bytes 16777216
  481.9 43.2 %copy.58 = f32[32,2,4,2,8,512]{5,3,2,0,4,1:T(2,128)} copy(f32[32,2,4,2,8,512]{0,3,2,1,5,4:T(2,128)} %bitcast.130) | data formatting | bytes 16777216 | tf_op jit(solution)/shard_map/all_to_all | solution.py:133
  525.1 11.9 %reshape.182 = f32[256,2,4096]{2,0,1:T(8,128)} reshape(f32[8,32,2,4,2,512]{5,4,3,1,0,2:T(2,128)} %bitcast.131) | data formatting | bytes 16777216 | tf_op jit(solution)/shard_map/reshape | solution.py:134
  537.0 7.4 %fusion.10 = f32[256,4096]{1,0:T(8,128)S(1)} fusion(f32[256,2,4096]{2,0,1:T(8,128)} %reshape.182, s32[256]{0:T(256)S(1)} %get-tuple-element.17, s32[256]{0:T(256)S(1)} %get-tuple-element.20, s32[256]{0:T(256)S(1)} %get-tuple-element.18, s32[256]{0:T(256)S(1)} %get-tuple-element.21, s32[256]{0:T(256)S(1)} %get-tuple-element.19, s32[256]{0:T(256)S(1)} %get-tuple-element.22), kind=kOutput, calls=%fused_computation.21 | convolution fusion | flops 3222601728 | bytes 8394752 | tf_op jit(solution)/shard_map/dot_general | solution.py:21
  544.4 5.2 fusion.11
  549.6 5.4 convolution_subtract_fusion
  555.0 5.2 convolution_add_fusion
  560.3 2.2 fusion.81
  562.5 2.4 fusion.79
  564.9 2.2 convolution_subtract_fusion.1
  567.2 0.2 stack.21
  567.5 4.4 convolution_add_fusion.1
  572.1 1.1 pad_maximum_fusion.1
  573.2 3.5 all-to-all-start.1
  577.4 9.0 %all-to-all-done.1 = f32[16,2,4,2,512]{4,3,2,1,0:T(2,128)S(1)} async-done(((f32[16,2,4,2,512]{4,3,2,1,0:T(2,128)}), f32[16,2,4,2,512]{4,3,2,1,0:T(2,128)S(1)}, u32[]{:S(2)}, u32[]{:S(2)}) %all-to-all-start.1) | async-done | bytes 524320 | tf_op jit(solution)/shard_map/all_to_all | solution.py:139
  586.4 0.3 copy.106
  586.9 0.6 fusion.40
  587.6 0.6 fusion.41
  588.2 0.6 convolution_add_fusion.2
  588.7 0.6 convolution_subtract_fusion.2
  589.4 0.6 fusion.49
  590.1 0.6 fusion.47
  590.7 0.7 fusion.33
  591.4 1.0 fusion.34
  592.5 11.7 %psum.7 = f32[2,64]{1,0:T(2,128)S(1)} all-reduce(f32[2,64]{1,0:T(2,128)S(1)} %fusion.34), channel_id=1, replica_groups=mesh['ka'=8,'pb'=4] {'pb'}, use_global_device_ids=true, to_apply=%region_1.2 | all-reduce | flops 128 | bytes 1024 | tf_op jit(solution)/shard_map/psum | solution.py:162
  604.2 0.6 broadcast_multiply_fusion
  (47 shorter events, 1.1 us)
Async XLA Ops:
  6.5 0.7 copy-start
  6.5 2.8 copy-start.5
  6.5 59.8 %all-gather.2.cloned.1.call-start = ((), (), s32[]{:S(2)}) async-start(), calls=%async_computation.2 | async-start | bytes 9437184 | tf_op jit(solution)/shard_map/all_gather | solution.py:117
  75.6 15.4 %slice-start = ((s8[8388608]{0:T(1024)(128)(4,1)}), s8[4194304]{0:T(1024)(128)(4,1)S(1)}, s32[]{:S(2)}) async-start(s8[8388608]{0:T(1024)(128)(4,1)} %bitcast.127), calls=%async_computation.3 | async-start | bytes 8388608
  85.9 5.1 slice-start.1
  91.0 21.9 %copy-start.3 = (f32[32,4,64,64,1]{3,0,2,1,4:T(8,128)}, f32[32,4,64,64,1]{3,0,2,1,4:T(8,128)S(1)}, u32[]{:S(2)}) copy-start(f32[32,4,64,64,1]{3,0,2,1,4:T(8,128)S(1)} %get-tuple-element.7) | copy-start | bytes 6291460
  298.7 5.1 copy-start.11
  298.7 99.2 %all-to-all-start = ((f32[8,1,262144]{2,1,0:T(1,128)}), f32[8,1,262144]{2,1,0:T(1,128)}, u32[]{:S(2)}, u32[]{:S(2)}) async-start(f32[8,1,262144]{2,1,0:T(1,128)} %reshape.195), calls=%async_computation | async-start | bytes 16777216 | tf_op jit(solution)/shard_map/all_to_all | solution.py:133
  537.0 7.4 %copy-start.2 = (f32[256,2,4096]{2,0,1:T(8,128)S(1)}, f32[256,2,4096]{2,0,1:T(8,128)}, u32[]{:S(2)}) copy-start(f32[256,2,4096]{2,0,1:T(8,128)} %reshape.182) | copy-start | bytes 25165828
  555.0 5.2 copy-start.4
  567.2 9.6 %copy-start.10 = (f32[4,2]{0,1:T(2,128)S(1)}, f32[4,2]{0,1:T(2,128)}, u32[]{:S(2)}) copy-start(f32[4,2]{0,1:T(2,128)} %param.19) | copy-start | bytes 100
  567.2 9.9 %copy-start.9 = (s32[2,4,64]{2,1,0:T(4,128)S(1)}, s32[2,4,64]{2,1,0:T(4,128)}, u32[]{:S(2)}) copy-start(s32[2,4,64]{2,1,0:T(4,128)} %param.18) | copy-start | bytes 6148
  567.2 10.0 %copy-start.8 = (f32[2,4,64]{2,1,0:T(4,128)S(1)}, f32[2,4,64]{2,1,0:T(4,128)}, u32[]{:S(2)}) copy-start(f32[2,4,64]{2,1,0:T(4,128)} %param.17) | copy-start | bytes 6148
  567.2 10.0 %copy-start.12 = (f32[2,64]{1,0:T(2,128)S(1)}, f32[2,64]{1,0:T(2,128)}, u32[]{:S(2)}) copy-start(f32[2,64]{1,0:T(2,128)} %param.16) | copy-start | bytes 1540
  567.4 19.5 %copy-start.7 = (f32[2,64,128]{2,1,0:T(8,128)S(1)}, f32[2,64,128]{2,1,0:T(8,128)}, u32[]{:S(2)}) copy-start(f32[2,64,128]{2,1,0:T(8,128)} %param.14) | copy-start | bytes 196612
  573.2 13.2 %all-to-all-start.1 = ((f32[16,2,4,2,512]{4,3,2,1,0:T(2,128)}), f32[16,2,4,2,512]{4,3,2,1,0:T(2,128)S(1)}, u32[]{:S(2)}, u32[]{:S(2)}) async-start(f32[16,2,4,2,512]{4,3,2,1,0:T(2,128)} %pad_maximum_fusion.1), calls=%async_computation.1 | async-start | bytes 1048576 | tf_op jit(solution)/shard_map/all_to_all | solution.py:139
  577.2 12.2 %copy-start.6 = (f32[2,4,64,128]{3,2,1,0:T(8,128)S(1)}, f32[2,4,64,128]{3,2,1,0:T(8,128)}, u32[]{:S(2)}) copy-start(f32[2,4,64,128]{3,2,1,0:T(8,128)} %param.15) | copy-start | bytes 786436
  590.0 14.7 %copy-start.1 = (s32[16,32]{1,0:T(8,128)S(1)}, s32[16,32]{1,0:T(8,128)}, u32[]{:S(2)}) copy-start(s32[16,32]{1,0:T(8,128)} %param.12) | copy-start | bytes 6148
Sparse Core Ops, SparseCore 0:
  9.2 57.0 all-gather.1
where the time goes:
time: 622 us; the launch traced here: 612 us
  local copies, waits for them, and re-layouts  236 us (38%)
  matrix products  152 us (24%)
  waiting for transfers between devices  150 us (24%)
  other arithmetic  40.2 us (6%)
  between operations  14 us (2%)
  blocking collectives  11.7 us (2%)
  starting transfers between devices  8.59 us (1%)
    dot_general x13, matrix products, mult(): return jnp.einsum(pattern, first, second, precision=PRECISE)  107 us
    all_to_all x1, waiting for transfers between devices, shards(): lax.all_to_all(pair_major, 'ka', split_axis=4, concat_axis=0, tiled=True)  94 us
    unnamed x33, local copies, waits for them, and re-layouts  90.6 us
    another operation x3, local copies, waits for them, and re-layouts, shards(): jnp.stack([wannier_real, wannier_imag], 1)  56.1 us
    all_gather x1, waiting for transfers between devices, shards(): lax.all_gather(gauge, 'ka', axis=0, tiled=True)  45.9 us
    dot_general x9, matrix products, product(): jnp.dot(left_matrix, right_matrix, precision=PRECISE, preferred_element_t...  44.9 us
    all_to_all x2, local copies, waits for them, and re-layouts, shards(): lax.all_to_all(pair_major, 'ka', split_axis=4, concat_axis=0, tiled=True)  43.7 us
    all_to_all x1, other arithmetic, shards(): lax.all_to_all(pair_major, 'ka', split_axis=4, concat_axis=0, tiled=True)  28.6 us
  transfers between devices with their start and end apart: 3, of which 3 were waited for; matrix products, arithmetic and copies ran while one was open for 2% of the time, Pallas kernels for 0%

commit v1 on v0

v1 whole, which is shorter than its diff:
```python
import functools
import math

import jax
import jax.numpy as jnp
from jax import lax
from jax.experimental import pallas as pl
from jax.experimental.pallas import tpu as pltpu
from jax.sharding import PartitionSpec as P

GX = 8
GY = 8
GZ = 4
FG = 32
NK = 256
BROADEN = 0.1
THERMAL = 0.05
VMEM_LIMIT = 48 * 1024 * 1024


def split(value):
    high = value.astype(jnp.bfloat16)
    low = (value - high.astype(jnp.float32)).astype(jnp.bfloat16)
    return high, low


def dot(first, second):
    return jnp.dot(first, second, preferred_element_type=jnp.float32)


def swap_halves(value, low_sign):
    half = value.shape[-1] // 2
    lane = lax.broadcasted_iota(jnp.int32, value.shape, value.ndim - 1)
    rolled = pltpu.roll(value, half, value.ndim - 1)
    return jnp.where(lane < half, low_sign * rolled, -low_sign * rolled)


def right_weights(matrix):
    block = jnp.concatenate([matrix, swap_halves(matrix, -1.0)], 0)
    high, low = split(block)
    row = jnp.concatenate([high, low], 1)
    return jnp.concatenate([row, row], 0)


def right_product(rows, weights):
    high, low = split(rows)
    wide = dot(jnp.concatenate([high, low], 1), weights)
    half = wide.shape[1] // 2
    return wide[:, :half] + wide[:, half:]


def left_weights(matrix):
    high, low = split(matrix)
    turned = jnp.concatenate([high, low], 0).T
    return jnp.concatenate([turned, turned], 1)


def left_product(turned, high, low):
    wide = dot(turned, jnp.concatenate([high, high, low, low], 0))
    half = wide.shape[0] // 2
    lanes = wide.shape[1] // 2
    parts = []
    for branch in range(2):
        piece = wide[:, branch * lanes : (branch + 1) * lanes]
        parts.append(piece[:half] + swap_halves(piece[half:], 1.0))
    return parts


def right_kernel(coupling_ref, gauge_ref, out_ref):
    points, qpoints, branches, orbitals, lanes = coupling_ref.shape
    for point in range(points):
        weights = right_weights(gauge_ref[point])
        rows = coupling_ref[point].reshape(qpoints * branches * orbitals, lanes)
        product = right_product(rows, weights)
        for q in range(qpoints):
            first = product[2 * q * orbitals : (2 * q + 1) * orbitals]
            second = product[(2 * q + 1) * orbitals : (2 * q + 2) * orbitals]
            high, low = split(jnp.concatenate([first, second], 1))
            out_ref[point, q, :orbitals] = high
            out_ref[point, q, orbitals:] = low


def left_kernel(index_ref, gauge_ref, right_ref, table_ref, out_ref, held_ref):
    points = right_ref.shape[0]
    _, orbitals, padded, _ = held_ref.shape
    fine = out_ref.shape[0]
    lanes = out_ref.shape[3]

    @pl.when(pl.program_id(0) == 0)
    def _():
        if padded != points:
            held_ref[...] = jnp.zeros_like(held_ref)

        @pl.loop(0, points, unroll=min(4, points))
        def _(point):
            turned = left_weights(gauge_ref[index_ref[point]])
            block = right_ref[point, 0]
            parts = left_product(turned, block[:orbitals], block[orbitals:])
            for branch in range(2):
                held_ref[branch, :, point, :] = parts[branch]

    t_high, t_low = split(table_ref[0])
    table = jnp.concatenate([t_high, t_high, t_low, t_low], 1)

    @pl.loop(0, orbitals, unroll=8)
    def _(row):
        high, low = split(jnp.concatenate([held_ref[0, row], held_ref[1, row]], 1))
        wide = dot(table, jnp.concatenate([high, low, high, low], 0))
        for branch in range(2):
            piece = wide[:, branch * lanes : (branch + 1) * lanes]
            out_ref[:, branch, row, :] = piece[:fine] + swap_halves(piece[fine:], -1.0)


def fine_kernel(scalars_ref, coupled_ref, right_ref, left_ref, energy_ref, gap_ref, filled_ref, out_ref):
    fine, qpoints, branches, orbitals, lanes = coupled_ref.shape
    for f in range(fine):
        weights = right_weights(right_ref[f])
        rows = coupled_ref[f].reshape(qpoints * branches * orbitals, lanes)
        product = right_product(rows, weights)
        total = jnp.zeros((orbitals, lanes), jnp.float32)
        energy = energy_ref[f : f + 1, :]
        for q in range(qpoints):
            first = product[2 * q * orbitals : (2 * q + 1) * orbitals]
            second = product[(2 * q + 1) * orbitals : (2 * q + 2) * orbitals]
            high, low = split(jnp.concatenate([first, second], 1))
            parts = left_product(left_weights(left_ref[f, q]), high, low)
            difference = energy - gap_ref[f, q]
            filled = filled_ref[f, q]
            for branch in range(branches):
                phonon = scalars_ref[0, q * branches + branch]
                bose = scalars_ref[1, q * branches + branch]
                scale = scalars_ref[2, q * branches + branch]
                square = parts[branch] * parts[branch]
                up = difference + phonon
                down = difference - phonon
                kernel = (bose + filled) * up / (up * up + BROADEN * BROADEN)
                kernel = kernel + (bose + 1.0 - filled) * down / (down * down + BROADEN * BROADEN)
                total = total + square * scale * kernel
        summed = jnp.sum(total, axis=0, keepdims=True)
        out_ref[f : f + 1, :] = summed + pltpu.roll(summed, lanes // 2, 1)


def axis_table(coords, places, cells):
    cell = jnp.arange(cells, dtype=jnp.int32) - cells // 2
    shift = coords[:, None] - places[None, :] * (FG // cells)
    index = (cell[:, None, None] * shift[None]) % FG
    angles = index.astype(jnp.float32) * (2.0 * math.pi / FG)
    return jnp.sum(jnp.cos(angles), 0) / cells, jnp.sum(jnp.sin(angles), 0) / cells


def times(first, second):
    return (
        first[0] * second[0] - first[1] * second[1],
        first[0] * second[1] + first[1] * second[0],
    )


def phase_table(fine_coords, points):
    first = axis_table(fine_coords[0], points // (GY * GZ), GX)
    second = axis_table(fine_coords[1], points // GZ % GY, GY)
    third = axis_table(fine_coords[2], points % GZ, GZ)
    return times(times(first, second), third)


def shards(
    coupling,
    gauge,
    kq_index,
    fine_coords,
    eig_right,
    eig_left,
    energy_k,
    energy_kq,
    occupied,
    frequency,
):
    points, qpoints, branches, orbitals, lanes = coupling.shape
    pb_count = lax.axis_size("pb")
    fine_total = fine_coords.shape[1]
    chunk = 16 if fine_total % 16 == 0 else fine_total
    chunks = fine_total // chunk
    padded = -(-points // 16) * 16
    params = pltpu.CompilerParams(vmem_limit_bytes=VMEM_LIMIT)

    all_gauge = lax.all_gather(gauge, "ka", axis=0, tiled=True)

    step = 4 if points % 4 == 0 else 1
    right = pl.pallas_call(
        right_kernel,
        grid=(points // step,),
        in_specs=[
            pl.BlockSpec((step, qpoints, branches, orbitals, lanes), lambda i: (i, 0, 0, 0, 0)),
            pl.BlockSpec((step, orbitals, lanes), lambda i: (i, 0, 0)),
        ],
        out_specs=pl.BlockSpec((step, qpoints, 2 * orbitals, 2 * lanes), lambda i: (i, 0, 0, 0)),
        out_shape=jax.ShapeDtypeStruct((points, qpoints, 2 * orbitals, 2 * lanes), jnp.bfloat16),
        compiler_params=params,
        cost_estimate=pl.CostEstimate(
            flops=8 * coupling.size * lanes, bytes_accessed=8 * coupling.size, transcendentals=0
        ),
        name="right_gauge",
    )(coupling, gauge)

    own_points = lax.axis_index("ka") * points + jnp.arange(points, dtype=jnp.int32)
    table_real, table_imag = phase_table(fine_coords, own_points)
    table = jnp.stack([table_real, table_imag]).reshape(2, chunks, chunk, points)
    table = table.transpose(1, 0, 2, 3).reshape(chunks, 2 * chunk, points)
    table = jnp.pad(table, ((0, 0), (0, 0), (0, padded - points)))
    own_rows = lax.dynamic_slice_in_dim(kq_index, lax.axis_index("pb") * qpoints, qpoints, 0)

    def one_qpoint(index, right_part, q):
        return pl.pallas_call(
            left_kernel,
            grid=(chunks,),
            in_specs=[
                pl.BlockSpec(memory_space=pltpu.SMEM),
                pl.BlockSpec(all_gauge.shape, lambda i: (0, 0, 0), pipeline_mode=pl.Buffered(1)),
                pl.BlockSpec((points, 1, 2 * orbitals, 2 * lanes), lambda i: (0, q, 0, 0)),
                pl.BlockSpec((1, 2 * chunk, padded), lambda i: (i, 0, 0)),
            ],
            out_specs=pl.BlockSpec((chunk, branches, orbitals, lanes), lambda i: (i, 0, 0, 0)),
            out_shape=jax.ShapeDtypeStruct((fine_total, branches, orbitals, lanes), jnp.float32),
            scratch_shapes=[pltpu.VMEM((branches, orbitals, padded, lanes), jnp.float32)],
            compiler_params=params,
            cost_estimate=pl.CostEstimate(
                flops=20_000_000_000, bytes_accessed=4 * all_gauge.size, transcendentals=0
            ),
            name="left_gauge",
        )(index, all_gauge, right_part, table)

    if chunks == 1:
        gathered = [
            lax.psum_scatter(one_qpoint(own_rows[q], right, q), "ka", scatter_dimension=0, tiled=True)
            for q in range(qpoints)
        ]
        coupled = jnp.stack(gathered, 1)
    else:

        def body(q, total):
            part = lax.dynamic_slice_in_dim(right, q, 1, 1)
            index = lax.dynamic_index_in_dim(own_rows, q, 0, keepdims=False)
            piece = lax.psum_scatter(
                one_qpoint(index, part, 0), "ka", scatter_dimension=0, tiled=True
            )
            return lax.dynamic_update_slice_in_dim(total, piece[:, None], q, 1)

        coupled = lax.fori_loop(
            0,
            qpoints,
            body,
            jnp.zeros((eig_right.shape[0], qpoints, branches, orbitals, lanes), jnp.float32),
        )

    phonon = frequency.reshape(-1)
    scalars = jnp.stack([phonon, 1.0 / (jnp.exp(phonon / THERMAL) - 1.0), 1.0 / (2.0 * phonon)])
    shape = eig_left.shape
    contrib = pl.pallas_call(
        fine_kernel,
        in_specs=[pl.BlockSpec(memory_space=pltpu.SMEM)]
        + [pl.BlockSpec(memory_space=pltpu.VMEM)] * 6,
        out_specs=pl.BlockSpec(memory_space=pltpu.VMEM),
        out_shape=jax.ShapeDtypeStruct((eig_right.shape[0], lanes), jnp.float32),
        compiler_params=params,
        name="fine_terms",
    )(
        scalars,
        coupled,
        eig_right,
        eig_left,
        jnp.concatenate([energy_k, energy_k], 1),
        jnp.broadcast_to(energy_kq[..., None], shape),
        jnp.broadcast_to(occupied.astype(jnp.float32)[..., None], shape),
    )
    summed = lax.psum(contrib[:, :orbitals], "pb")
    return summed / (qpoints * pb_count * orbitals)


def solution(mesh):
    in_specs = (
        P("ka", "pb", None, None, None),
        P("ka", None, None),
        P(None, "ka"),
        P(),
        P("ka", None, None),
        P("ka", "pb", None, None),
        P("ka", None),
        P("ka", "pb", None),
        P("ka", "pb", None),
        P("pb", None),
    )
    out_specs = P("ka", None)
    return jax.shard_map(shards, mesh=mesh, in_specs=in_specs, out_specs=out_specs, check_vma=False)
```

time: 622 us -> 254 us (0.41); the launches traced: 612 us -> 253 us
  local copies, waits for them, and re-layouts: 236 us -> 2.5 us
  matrix products: 152 us -> 0 us
  Pallas kernels: 0 us -> 58.9 us
  other arithmetic: 40.2 us -> 2.91 us
  waiting for transfers between devices: 150 us -> 164 us
  starting transfers between devices: 8.59 us -> 0.17 us
    dot_general x22 -> x0, matrix products: 152 us -> none  [the longest x13 107 us: mult(): return jnp.einsum(pattern, first, second, precision=PRECISE)]
    reduce_scatter x0 -> x4, waiting for transfers between devices: none -> 118 us  [shards(): lax.psum_scatter(one_qpoint(own_rows[q], right, q), 'ka', scatter_dimensi...]
    all_to_all x2 -> x0, waiting for transfers between devices: 103 us -> none  [the longest x1 94 us: shards(): lax.all_to_all(pair_major, 'ka', split_axis=4, concat_axis=0, tiled=True)]
    unnamed x33 -> x17, local copies, waits for them, and re-layouts: 90.6 us -> 1.36 us
    pallas_call x0 -> x6, Pallas kernels: none -> 58.9 us  [the longest x4 46.6 us: one_qpoint(): pl.pallas_call(left_kernel, grid=(chunks,), in_specs=[pl.BlockSpec(memory...]
    another operation x5 -> x1, local copies, waits for them, and re-layouts: 56.6 us -> 0.09 us  [shards(): jnp.stack([phonon, 1.0 / (jnp.exp(phonon / THERMAL) - 1.0), 1.0 / (2.0 *...]
    all_to_all x3 -> x0, local copies, waits for them, and re-layouts: 44 us -> none  [the longest x2 43.7 us: shards(): lax.all_to_all(pair_major, 'ka', split_axis=4, concat_axis=0, tiled=True)]
    all_to_all x1 -> x0, other arithmetic: 28.6 us -> none  [shards(): lax.all_to_all(pair_major, 'ka', split_axis=4, concat_axis=0, tiled=True)]
  transfers between devices with their start and end apart: 3 -> 5, of which waited for: 3 -> 5; matrix products, arithmetic and copies ran while one was open for 2% -> 1% of each run, Pallas kernels for 0% -> 18%
where the time goes in v1:
time: 254 us; the launch traced here: 253 us
  waiting for transfers between devices  164 us (65%)
  Pallas kernels  58.9 us (23%)
  between operations  13.3 us (5%)
  blocking collectives  11.7 us (5%)
  other arithmetic  2.91 us (1%)
    reduce_scatter x4, waiting for transfers between devices, shards(): lax.psum_scatter(one_qpoint(own_rows[q], right, q), 'ka', scatter_dimensi...  118 us
    pallas_call x4, Pallas kernels, one_qpoint(): pl.pallas_call(left_kernel, grid=(chunks,), in_specs=[pl.BlockSpec(memory...  46.6 us
    all_gather x1, waiting for transfers between devices, shards(): all_gauge = lax.all_gather(gauge, 'ka', axis=0, tiled=True)  45 us
    psum x1, blocking collectives, shards(): summed = lax.psum(contrib[:, :orbitals], 'pb')  11.7 us
    pallas_call x1, Pallas kernels, shards(): pl.pallas_call(right_kernel, grid=(points // step,), in_specs=[pl.BlockSp...  10.9 us
  transfers between devices with their start and end apart: 5, of which 5 were waited for; matrix products, arithmetic and copies ran while one was open for 1% of the time, Pallas kernels for 18%

profile of v1, /device:TPU:0, one launch (start us, length us, event | category | flops | bytes accessed | tf_op | source)
XLA Modules:
  0.0 253.2 jit_solution(12159717504393855149)
XLA Ops:
  6.5 0.0 copy-start
  6.5 0.0 all-gather.2.cloned.1.call-start
  6.5 0.7 all-gather.2.cloned.1.call-update
  7.3 0.0 reduce-scatter.9.cloned.1.call-start
  7.4 0.0 copy-done
  7.4 0.8 slice_bitcast_fusion.4
  8.2 0.1 broadcast_subtract_fusion
  8.3 0.2 cosine_reduce_fusion.2
  8.5 0.1 broadcast_subtract_fusion.1
  8.6 0.1 broadcast_subtract_fusion.2
  8.6 0.6 cosine_reduce_fusion.1
  9.3 0.0 copy-start.1
  9.3 1.2 copy-done.1
  10.5 10.9 %right_gauge.1.right_ref = bf16[32,4,128,256]{3,2,1,0:T(8,128)(2,1)} custom-call(f32[32,4,2,64,128]{4,3,2,1,0:T(8,128)} %coupling_ref.1, f32[32,64,128]{2,1,0:T(8,128)S(1)} %copy-done.1), custom_call_target="tpu_custom_call" | custom-call | flops 2147483648 | bytes 16777216 | tf_op jit(solution)/shard_map/right_gauge/pallas_call | solution.py:188
  21.4 45.0 %all-gather.2.cloned.1.call-done.gauge_ref = f32[256,64,128]{2,1,0:T(8,128)} async-done(((f32[32,64,128]{2,1,0:T(8,128)}), f32[256,64,128]{2,1,0:T(8,128)}) %all-gather.2.cloned.1.call-update) | async-done | bytes 8388624 | tf_op jit(solution)/shard_map/all_gather | solution.py:185
  66.4 11.6 %left_gauge.6 = f32[16,2,64,128]{3,2,1,0:T(8,128)} custom-call(s32[32]{0:T(128)S(1)} %get-tuple-element.18.index_ref, f32[256,64,128]{2,1,0:T(8,128)} %all-gather.2.cloned.1.call-done.gauge_ref, bf16[32,4,128,256]{3,2,1,0:T(8,128)(2,1)} %right_gauge.1.right_ref, f32[1,32,32]{2,1,0:T(8,128)S(1)} %bitcast.24), custom_call_target="tpu_custom_call" | custom-call | flops 20000000000 | bytes 8388608 | tf_op jit(solution)/shard_map/left_gauge/pallas_call | solution.py:212
  78.0 0.0 reduce-scatter.9.cloned.1.call-update
  78.0 0.0 reduce-scatter.5.cloned.1.call-start
  78.0 11.6 %left_gauge.4 = f32[16,2,64,128]{3,2,1,0:T(8,128)} custom-call(s32[32]{0:T(128)S(1)} %get-tuple-element.16.index_ref, f32[256,64,128]{2,1,0:T(8,128)} %all-gather.2.cloned.1.call-done.gauge_ref, bf16[32,4,128,256]{3,2,1,0:T(8,128)(2,1)} %right_gauge.1.right_ref, f32[1,32,32]{2,1,0:T(8,128)S(1)} %bitcast.25), custom_call_target="tpu_custom_call" | custom-call | flops 20000000000 | bytes 8388608 | tf_op jit(solution)/shard_map/left_gauge/pallas_call | solution.py:212
  89.7 0.0 reduce-scatter.5.cloned.1.call-update
  89.7 0.0 reduce-scatter.7.cloned.1.call-start
  89.7 11.6 %left_gauge.5 = f32[16,2,64,128]{3,2,1,0:T(8,128)} custom-call(s32[32]{0:T(128)S(1)} %get-tuple-element.19.index_ref, f32[256,64,128]{2,1,0:T(8,128)} %all-gather.2.cloned.1.call-done.gauge_ref, bf16[32,4,128,256]{3,2,1,0:T(8,128)(2,1)} %right_gauge.1.right_ref, f32[1,32,32]{2,1,0:T(8,128)S(1)} %bitcast.26), custom_call_target="tpu_custom_call" | custom-call | flops 20000000000 | bytes 8388608 | tf_op jit(solution)/shard_map/left_gauge/pallas_call | solution.py:212
  101.4 0.0 reduce-scatter.7.cloned.1.call-update
  101.4 0.0 reduce-scatter.11.cloned.1.call-start
  101.4 0.0 copy-start.6
  101.4 0.0 copy-start.5
  101.5 0.0 copy-start.7
  101.5 0.0 copy-start.4
  101.5 0.0 copy-start.2
  101.5 0.0 copy-start.3
  101.5 11.7 %left_gauge.7 = f32[16,2,64,128]{3,2,1,0:T(8,128)} custom-call(s32[32]{0:T(128)S(1)} %get-tuple-element.17.index_ref, f32[256,64,128]{2,1,0:T(8,128)} %all-gather.2.cloned.1.call-done.gauge_ref, bf16[32,4,128,256]{3,2,1,0:T(8,128)(2,1)} %right_gauge.1.right_ref, f32[1,32,32]{2,1,0:T(8,128)S(1)} %bitcast.27), custom_call_target="tpu_custom_call" | custom-call | flops 20000000000 | bytes 8388608 | tf_op jit(solution)/shard_map/left_gauge/pallas_call | solution.py:212
  113.3 0.0 reduce-scatter.11.cloned.1.call-update
  113.3 0.0 copy-done.6
  113.3 0.1 copy.14
  113.4 0.1 stack_reshape.3
  113.5 0.0 copy-done.5
  113.5 0.0 copy-done.7
  113.5 0.1 pad_maximum_fusion.3.energy_ref
  113.6 0.6 reduce-scatter.9.cloned.1.call-done
  114.2 39.2 %reduce-scatter.5.cloned.1.call-done = f32[2,2,64,128]{3,2,1,0:T(8,128)} async-done(((f32[16,2,64,128]{3,2,1,0:T(8,128)}), f32[2,2,64,128]{3,2,1,0:T(8,128)}) %reduce-scatter.5.cloned.1.call-update) | async-done | bytes 131088 | tf_op jit(solution)/shard_map/reduce_scatter | solution.py:233
  153.4 39.1 %reduce-scatter.7.cloned.1.call-done = f32[2,2,64,128]{3,2,1,0:T(8,128)} async-done(((f32[16,2,64,128]{3,2,1,0:T(8,128)}), f32[2,2,64,128]{3,2,1,0:T(8,128)}) %reduce-scatter.7.cloned.1.call-update) | async-done | bytes 131088 | tf_op jit(solution)/shard_map/reduce_scatter | solution.py:233
  192.5 39.1 %reduce-scatter.11.cloned.1.call-done = f32[2,2,64,128]{3,2,1,0:T(8,128)} async-done(((f32[16,2,64,128]{3,2,1,0:T(8,128)}), f32[2,2,64,128]{3,2,1,0:T(8,128)}) %reduce-scatter.11.cloned.1.call-update) | async-done | bytes 131088 | tf_op jit(solution)/shard_map/reduce_scatter | solution.py:233
  231.5 1.1 pad_maximum_fusion.coupled_ref
  232.7 0.1 broadcast_in_dim.5.filled_ref
  232.8 0.1 broadcast_in_dim.4.gap_ref
  233.0 1.5 fine_terms.1
  234.4 11.7 %psum.7 = f32[2,64]{1,0:T(2,128)S(1)} all-reduce(f32[2,64]{1,0:T(2,128)S(1)} %bitcast.28), channel_id=1, replica_groups=mesh['ka'=8,'pb'=4] {'pb'}, use_global_device_ids=true, to_apply=%region_10.11 | all-reduce | flops 128 | bytes 1024 | tf_op jit(solution)/shard_map/psum | solution.py:274
  246.1 0.6 broadcast_multiply_fusion
  (15 shorter events, 0.1 us)
Async XLA Ops:
  6.5 0.8 copy-start
  6.5 59.8 %all-gather.2.cloned.1.call-start = ((), (), s32[]{:S(2)}) async-start(), calls=%async_computation.4 | async-start | bytes 9437184 | tf_op jit(solution)/shard_map/all_gather | solution.py:185
  7.3 106.9 %reduce-scatter.9.cloned.1.call-start = ((), (), s32[]{:S(2)}) async-start(), calls=%async_computation.7 | async-start | bytes 1179648 | tf_op jit(solution)/shard_map/reduce_scatter | solution.py:233
  9.3 1.2 copy-start.1
  78.0 75.4 %reduce-scatter.5.cloned.1.call-start = ((), (), s32[]{:S(2)}) async-start(), calls=%async_computation.5 | async-start | bytes 1179648 | tf_op jit(solution)/shard_map/reduce_scatter | solution.py:233
  89.7 102.8 %reduce-scatter.7.cloned.1.call-start = ((), (), s32[]{:S(2)}) async-start(), calls=%async_computation.6 | async-start | bytes 1179648 | tf_op jit(solution)/shard_map/reduce_scatter | solution.py:233
  101.4 130.1 %reduce-scatter.11.cloned.1.call-start = ((), (), s32[]{:S(2)}) async-start(), calls=%async_computation.8 | async-start | bytes 1179648 | tf_op jit(solution)/shard_map/reduce_scatter | solution.py:233
  101.4 11.8 %copy-start.6 = (f32[4,2]{0,1:T(2,128)S(1)}, f32[4,2]{0,1:T(2,128)}, u32[]{:S(2)}) copy-start(f32[4,2]{0,1:T(2,128)} %param.19) | copy-start | bytes 100
  101.4 12.0 %copy-start.5 = (s32[2,4,64]{2,1,0:T(4,128)S(1)}, s32[2,4,64]{2,1,0:T(4,128)}, u32[]{:S(2)}) copy-start(s32[2,4,64]{2,1,0:T(4,128)} %param.18) | copy-start | bytes 6148
  101.5 12.0 %copy-start.7 = (f32[2,64]{1,0:T(2,128)S(1)}, f32[2,64]{1,0:T(2,128)}, u32[]{:S(2)}) copy-start(f32[2,64]{1,0:T(2,128)} %param.16) | copy-start | bytes 1540
  101.5 131.3 %copy-start.4 = (f32[2,4,64]{2,1,0:T(4,128)S(1)}, f32[2,4,64]{2,1,0:T(4,128)}, u32[]{:S(2)}) copy-start(f32[2,4,64]{2,1,0:T(4,128)} %param.17) | copy-start | bytes 6148
  101.5 131.5 %copy-start.2 = (f32[2,4,64,128]{3,2,1,0:T(8,128)S(1)}, f32[2,4,64,128]{3,2,1,0:T(8,128)}, u32[]{:S(2)}) copy-start(f32[2,4,64,128]{3,2,1,0:T(8,128)} %left_ref.1) | copy-start | bytes 786436
  101.5 131.4 %copy-start.3 = (f32[2,64,128]{2,1,0:T(8,128)S(1)}, f32[2,64,128]{2,1,0:T(8,128)}, u32[]{:S(2)}) copy-start(f32[2,64,128]{2,1,0:T(8,128)} %right_ref.1) | copy-start | bytes 196612
Sparse Core Ops, SparseCore 0:
  9.2 57.0 all-gather.1
  78.1 36.0 reduce-scatter.8
  117.3 36.0 reduce-scatter.4
  156.4 35.9 reduce-scatter.6
  195.5 35.9 reduce-scatter.10

commit v2 on v1

--- a/solution.py
+++ b/solution.py
@@ -16,6 +16,7 @@
 BROADEN = 0.1
 THERMAL = 0.05
 VMEM_LIMIT = 48 * 1024 * 1024
+UNROLL = 4
 
 
 def split(value):
@@ -140,6 +141,134 @@
         out_ref[f : f + 1, :] = summed + pltpu.roll(summed, lanes // 2, 1)
 
 
+def window_kernel(
+    index_ref, scalars_ref, gauge_ref, right_ref, table_ref, fine_right_ref, fine_left_ref,
+    energy_ref, gap_ref, filled_ref, out_ref,
+    held_ref, partial_ref, arrived_ref, total_ref, terms_ref, others_ref,
+    send_sem, recv_sem, terms_send, terms_recv,
+):
+    points, qpoints = right_ref.shape[0], right_ref.shape[1]
+    branches, orbitals, padded, lanes = held_ref.shape
+    fine_total = partial_ref.shape[1]
+    fine = fine_right_ref.shape[0]
+    ka_count, pb_count = lax.axis_size("ka"), lax.axis_size("pb")
+    me, layer = lax.axis_index("ka"), lax.axis_index("pb")
+
+    def ka_device(offset):
+        return (lax.rem(me + offset, ka_count), layer)
+
+    def pb_device(offset):
+        return (me, lax.rem(layer + offset, pb_count))
+
+    barrier = pltpu.get_barrier_semaphore()
+    for offset in range(1, ka_count):
+        pl.semaphore_signal(
+            barrier, inc=1, device_id=ka_device(offset), device_id_type=pl.DeviceIdType.MESH
+        )
+    for offset in range(1, pb_count):
+        pl.semaphore_signal(
+            barrier, inc=1, device_id=pb_device(offset), device_id_type=pl.DeviceIdType.MESH
+        )
+    pl.semaphore_wait(barrier, ka_count + pb_count - 2)
+
+    def piece(q, offset):
+        target = lax.rem(me + offset, ka_count)
+        return pltpu.make_async_remote_copy(
+            src_ref=partial_ref.at[q, pl.ds(target * fine, fine)],
+            dst_ref=arrived_ref.at[q, offset - 1],
+            send_sem=send_sem.at[q, offset - 1],
+            recv_sem=recv_sem.at[q, offset - 1],
+            device_id=(target, layer),
+            device_id_type=pl.DeviceIdType.MESH,
+        )
+
+    total_ref[...] = jnp.zeros_like(total_ref)
+    terms_ref[...] = jnp.zeros_like(terms_ref)
+    if padded != points:
+        held_ref[...] = jnp.zeros_like(held_ref)
+
+    @pl.loop(0, qpoints + 1)
+    def _(q):
+        @pl.when(q < qpoints)
+        def _():
+            @pl.loop(0, points, unroll=min(UNROLL, points))
+            def _(point):
+                turned = left_weights(gauge_ref[index_ref[q * points + point]])
+                block = right_ref[point, q]
+                parts = left_product(turned, block[:orbitals], block[orbitals:])
+                for branch in range(2):
+                    held_ref[branch, :, point, :] = parts[branch]
+
+            t_high, t_low = split(table_ref[...])
+            table = jnp.concatenate([t_high, t_high, t_low, t_low], 1)
+
+            @pl.loop(0, orbitals, unroll=8)
+            def _(row):
+                high, low = split(jnp.concatenate([held_ref[0, row], held_ref[1, row]], 1))
+                wide = dot(table, jnp.concatenate([high, low, high, low], 0))
+                for branch in range(2):
+                    part = wide[:, branch * lanes : (branch + 1) * lanes]
+                    partial_ref[q, :, branch, row, :] = part[:fine_total] + swap_halves(
+                        part[fine_total:], -1.0
+                    )
+
+            for offset in range(1, ka_count):
+                piece(q, offset).start()
+
+        @pl.when(q > 0)
+        def _():
+            done = q - 1
+            for offset in range(1, ka_count):
+                piece(done, offset).wait()
+            for f in range(fine):
+                rows = partial_ref[done, me * fine + f]
+                for offset in range(1, ka_count):
+                    rows = rows + arrived_ref[done, offset - 1, f]
+                product = right_product(
+                    rows.reshape(branches * orbitals, lanes), right_weights(fine_right_ref[f])
+                )
+                high, low = split(jnp.concatenate([product[:orbitals], product[orbitals:]], 1))
+                parts = left_product(left_weights(fine_left_ref[f, done]), high, low)
+                difference = energy_ref[f : f + 1, :] - gap_ref[f, done]
+                filled = filled_ref[f, done]
+                total = total_ref[f]
+                for branch in range(branches):
+                    phonon = scalars_ref[0, done * branches + branch]
+                    bose = scalars_ref[1, done * branches + branch]
+                    scale = scalars_ref[2, done * branches + branch]
+                    square = parts[branch] * parts[branch]
+                    up = difference + phonon
+                    down = difference - phonon
+                    kernel = (bose + filled) * up / (up * up + BROADEN * BROADEN)
+                    kernel = kernel + (bose + 1.0 - filled) * down / (
+                        down * down + BROADEN * BROADEN
+                    )
+                    total = total + square * scale * kernel
+                total_ref[f] = total
+
+    for f in range(fine):
+        summed = jnp.sum(total_ref[f], axis=0, keepdims=True)
+        terms_ref[f : f + 1, :] = summed + pltpu.roll(summed, lanes // 2, 1)
+    copies = []
+    for offset in range(1, pb_count):
+        copies.append(
+            pltpu.make_async_remote_copy(
+                src_ref=terms_ref,
+                dst_ref=others_ref.at[offset - 1],
+                send_sem=terms_send.at[offset - 1],
+                recv_sem=terms_recv.at[offset - 1],
+                device_id=pb_device(offset),
+                device_id_type=pl.DeviceIdType.MESH,
+            )
+        )
+        copies[-1].start()
+    summed = terms_ref[...]
+    for offset in range(1, pb_count):
+        copies[offset - 1].wait()
+        summed = summed + others_ref[offset - 1]
+    out_ref[...] = summed[:fine] / (qpoints * pb_count * orbitals)
+
+
 def axis_table(coords, places, cells):
     cell = jnp.arange(cells, dtype=jnp.int32) - cells // 2
     shift = coords[:, None] - places[None, :] * (FG // cells)
@@ -208,6 +337,48 @@
     table = jnp.pad(table, ((0, 0), (0, 0), (0, padded - points)))
     own_rows = lax.dynamic_slice_in_dim(kq_index, lax.axis_index("pb") * qpoints, qpoints, 0)
 
+    phonon = frequency.reshape(-1)
+    scalars = jnp.stack([phonon, 1.0 / (jnp.exp(phonon / THERMAL) - 1.0), 1.0 / (2.0 * phonon)])
+    shape = eig_left.shape
+    energy_lanes = jnp.concatenate([energy_k, energy_k], 1)
+    gap_lanes = jnp.broadcast_to(energy_kq[..., None], shape)
+    filled_lanes = jnp.broadcast_to(occupied.astype(jnp.float32)[..., None], shape)
+
+    ka_count = lax.axis_size("ka")
+    fine_rows = eig_right.shape[0]
+    fine_rows_padded = -(-fine_rows // 8) * 8
+    partial_size = fine_total * branches * orbitals * lanes * 4 * qpoints
+    if chunks == 1 and ka_count > 1 and pb_count > 1 and partial_size <= 8 * 1024 * 1024:
+        ka_others, pb_others = ka_count - 1, pb_count - 1
+        vmem = pl.BlockSpec(memory_space=pltpu.VMEM)
+        smem = pl.BlockSpec(memory_space=pltpu.SMEM)
+        summed = pl.pallas_call(
+            window_kernel,
+            in_specs=[smem, smem] + [vmem] * 8,
+            out_specs=vmem,
+            out_shape=jax.ShapeDtypeStruct((fine_rows, lanes), jnp.float32),
+            scratch_shapes=[
+                pltpu.VMEM((branches, orbitals, padded, lanes), jnp.float32),
+                pltpu.VMEM((qpoints, fine_total, branches, orbitals, lanes), jnp.float32),
+                pltpu.VMEM((qpoints, ka_others, fine_rows, branches, orbitals, lanes), jnp.float32),
+                pltpu.VMEM((fine_rows, orbitals, lanes), jnp.float32),
+                pltpu.VMEM((fine_rows_padded, lanes), jnp.float32),
+                pltpu.VMEM((pb_others, fine_rows_padded, lanes), jnp.float32),
+                pltpu.SemaphoreType.DMA((qpoints, ka_others)),
+                pltpu.SemaphoreType.DMA((qpoints, ka_others)),
+                pltpu.SemaphoreType.DMA((pb_others,)),
+                pltpu.SemaphoreType.DMA((pb_others,)),
+            ],
+            compiler_params=pltpu.CompilerParams(
+                vmem_limit_bytes=VMEM_LIMIT, collective_id=0, has_side_effects=True
+            ),
+            name="window",
+        )(
+            own_rows.reshape(-1), scalars, all_gauge, right, table[0], eig_right, eig_left,
+            energy_lanes, gap_lanes, filled_lanes,
+        )
+        return summed[:, :orbitals]
+
     def one_qpoint(index, right_part, q):
         return pl.pallas_call(
             left_kernel,
@@ -251,9 +422,6 @@
             jnp.zeros((eig_right.shape[0], qpoints, branches, orbitals, lanes), jnp.float32),
         )
 
-    phonon = frequency.reshape(-1)
-    scalars = jnp.stack([phonon, 1.0 / (jnp.exp(phonon / THERMAL) - 1.0), 1.0 / (2.0 * phonon)])
-    shape = eig_left.shape
     contrib = pl.pallas_call(
         fine_kernel,
         in_specs=[pl.BlockSpec(memory_space=pltpu.SMEM)]
@@ -267,9 +435,9 @@
         coupled,
         eig_right,
         eig_left,
-        jnp.concatenate([energy_k, energy_k], 1),
-        jnp.broadcast_to(energy_kq[..., None], shape),
-        jnp.broadcast_to(occupied.astype(jnp.float32)[..., None], shape),
+        energy_lanes,
+        gap_lanes,
+        filled_lanes,
     )
     summed = lax.psum(contrib[:, :orbitals], "pb")
     return summed / (qpoints * pb_count * orbitals)

time: 254 us -> 140 us (0.55)
  waiting for transfers between devices: 164 us -> 43.1 us
  Pallas kernels: 58.9 us -> 76.6 us
  blocking collectives: 11.7 us -> 0 us
    reduce_scatter x4 -> x0, waiting for transfers between devices: 118 us -> none  [shards(): lax.psum_scatter(one_qpoint(own_rows[q], right, q), 'ka', scatter_dimensi...]
    pallas_call x5 -> x1, Pallas kernels: 48.1 us -> 65.6 us  [shards(): pl.pallas_call(window_kernel, in_specs=[smem, smem] + [vmem] * 8, out_spe...]
    psum x1 -> x0, blocking collectives: 11.7 us -> none  [shards(): summed = lax.psum(contrib[:, :orbitals], 'pb')]
  transfers between devices with their start and end apart: 5 -> 1, of which waited for: 5 -> 1; matrix products, arithmetic and copies ran while one was open for 1% -> 3% of each run, Pallas kernels for 18% -> 8%
where the time goes in v2:
time: 140 us
  Pallas kernels  76.6 us (55%)
  waiting for transfers between devices  43.1 us (31%)
  between operations  13.5 us (10%)
  local copies, waits for them, and re-layouts  3.79 us (3%)
  other arithmetic  2.66 us (2%)
    pallas_call x1, Pallas kernels, shards(): pl.pallas_call(window_kernel, in_specs=[smem, smem] + [vmem] * 8, out_spe...  65.6 us
    all_gather x1, waiting for transfers between devices, shards(): all_gauge = lax.all_gather(gauge, 'ka', axis=0, tiled=True)  42.4 us
    pallas_call x1, Pallas kernels, shards(): pl.pallas_call(right_kernel, grid=(points // step,), in_specs=[pl.BlockSp...  11 us
  transfers between devices with their start and end apart: 1, of which 1 were waited for; matrix products, arithmetic and copies ran while one was open for 3% of the time, Pallas kernels for 8%

profile of v2, /device:TPU:0, one launch (start us, length us, event | category | flops | bytes accessed | tf_op | source)
XLA Modules:
  0.0 139.7 jit_solution(9244928463884633176)
XLA Ops:
  6.5 0.0 copy-start
  6.5 0.0 all-gather.2.cloned.1.call-start
  6.5 0.7 all-gather.2.cloned.1.call-update
  7.3 0.0 copy-done
  7.3 0.1 reshape.316.index_ref
  7.4 0.8 copy.14
  8.1 0.1 stack_reshape.3
  8.2 0.7 convert_element_type.15
  9.0 0.8 pad_maximum_fusion.2.energy_ref
  9.8 0.8 slice_bitcast_fusion.1
  10.6 0.1 broadcast_subtract_fusion
  10.7 0.2 cosine_reduce_fusion.2
  10.9 0.1 broadcast_subtract_fusion.1
  11.0 0.1 broadcast_subtract_fusion.2
  11.1 0.6 cosine_reduce_fusion.1
  11.7 0.0 copy-start.1
  11.7 1.2 copy-done.1
  13.0 0.0 copy-start.4
  13.0 0.0 copy-start.2
  13.0 0.0 copy-start.3
  13.0 11.0 %right_gauge.1.right_ref = bf16[32,4,128,256]{3,2,1,0:T(8,128)(2,1)} custom-call(f32[32,4,2,64,128]{4,3,2,1,0:T(8,128)} %coupling_ref.1, f32[32,64,128]{2,1,0:T(8,128)S(1)} %copy-done.1), custom_call_target="tpu_custom_call" | custom-call | flops 2147483648 | bytes 16777216 | tf_op jit(solution)/shard_map/right_gauge/pallas_call | solution.py:317
  23.9 42.4 %all-gather.2.cloned.1.call-done.gauge_ref = f32[256,64,128]{2,1,0:T(8,128)} async-done(((f32[32,64,128]{2,1,0:T(8,128)}), f32[256,64,128]{2,1,0:T(8,128)}) %all-gather.2.cloned.1.call-update) | async-done | bytes 8388624 | tf_op jit(solution)/shard_map/all_gather | solution.py:314
  66.4 0.1 broadcast_in_dim.5.filled_ref
  66.5 0.0 copy-done.4
  66.5 0.1 broadcast_in_dim.4.gap_ref
  66.6 0.0 copy-done.2
  66.6 0.0 copy-done.3
  66.7 65.6 %window.1 = f32[2,128]{1,0:T(2,128)S(1)} custom-call(s32[128]{0:T(128)S(1)} %reshape.316.index_ref, f32[3,8]{1,0:T(4,128)S(1)} %pad_maximum_fusion.1.scalars_ref, f32[256,64,128]{2,1,0:T(8,128)} %all-gather.2.cloned.1.call-done.gauge_ref, bf16[32,4,128,256]{3,2,1,0:T(8,128)(2,1)} %right_gauge.1.right_ref, f32[32,32]{1,0:T(8,128)S(1)} %bitcast.12, ...), custom_call_target="tpu_custom_call" | custom-call | tf_op jit(solution)/shard_map/window/pallas_call | solution.py:355
  132.3 0.6 copy.16
  (10 shorter events, 0.1 us)
Async XLA Ops:
  6.5 0.7 copy-start
  6.5 59.8 %all-gather.2.cloned.1.call-start = ((), (), s32[]{:S(2)}) async-start(), calls=%async_computation | async-start | bytes 9437184 | tf_op jit(solution)/shard_map/all_gather | solution.py:314
  11.7 1.2 copy-start.1
  13.0 53.5 %copy-start.4 = (f32[2,4,64]{2,1,0:T(4,128)S(1)}, f32[2,4,64]{2,1,0:T(4,128)}, u32[]{:S(2)}) copy-start(f32[2,4,64]{2,1,0:T(4,128)} %param.17) | copy-start | bytes 6148
  13.0 53.7 %copy-start.2 = (f32[2,4,64,128]{3,2,1,0:T(8,128)S(1)}, f32[2,4,64,128]{3,2,1,0:T(8,128)}, u32[]{:S(2)}) copy-start(f32[2,4,64,128]{3,2,1,0:T(8,128)} %fine_left_ref.1) | copy-start | bytes 786436
  13.0 53.7 %copy-start.3 = (f32[2,64,128]{2,1,0:T(8,128)S(1)}, f32[2,64,128]{2,1,0:T(8,128)}, u32[]{:S(2)}) copy-start(f32[2,64,128]{2,1,0:T(8,128)} %fine_right_ref.1) | copy-start | bytes 196612
Sparse Core Ops, SparseCore 0:
  9.2 57.0 all-gather.1

commit v3 on v2

--- a/solution.py
+++ b/solution.py
@@ -142,11 +142,14 @@
 
 
 def window_kernel(
-    index_ref, scalars_ref, gauge_ref, right_ref, table_ref, fine_right_ref, fine_left_ref,
+    index_ref, scalars_ref, own_ref, coupling_ref, table_ref, fine_right_ref, fine_left_ref,
     energy_ref, gap_ref, filled_ref, out_ref,
     held_ref, partial_ref, arrived_ref, total_ref, terms_ref, others_ref,
     send_sem, recv_sem, terms_send, terms_recv,
+    gauge_ref, coupled_ref, right_ref, gather_send, gather_recv, load_sem,
 ):
+    load = pltpu.make_async_copy(coupling_ref, coupled_ref, load_sem)
+    load.start()
     points, qpoints = right_ref.shape[0], right_ref.shape[1]
     branches, orbitals, padded, lanes = held_ref.shape
     fine_total = partial_ref.shape[1]
@@ -160,6 +163,7 @@
     def pb_device(offset):
         return (me, lax.rem(layer + offset, pb_count))
 
+    gauge_ref[pl.ds(me * points, points)] = own_ref[...]
     barrier = pltpu.get_barrier_semaphore()
     for offset in range(1, ka_count):
         pl.semaphore_signal(
@@ -170,6 +174,64 @@
             barrier, inc=1, device_id=pb_device(offset), device_id_type=pl.DeviceIdType.MESH
         )
     pl.semaphore_wait(barrier, ka_count + pb_count - 2)
+
+    bits = [1 << b for b in range(1, ka_count.bit_length() - 1)]
+    orders = (bits + [1], bits[::-1] + [1])
+    half = points // 2
+
+    def last_bit(stream, mask):
+        return [bit for bit in orders[stream] if mask & bit][-1]
+
+    def flipped(mask):
+        place = me
+        for bit in orders[0]:
+            if mask & bit:
+                place = place + bit - 2 * bit * lax.rem(me // bit, 2)
+        return place
+
+    def block(stream, mask):
+        bit = last_bit(stream, mask)
+        rows = pl.ds(flipped(mask - bit) * points + stream * half, half)
+        return pltpu.make_async_remote_copy(
+            src_ref=gauge_ref.at[rows],
+            dst_ref=gauge_ref.at[rows],
+            send_sem=gather_send.at[stream, mask - 1],
+            recv_sem=gather_recv.at[stream, mask - 1],
+            device_id=(flipped(bit), layer),
+            device_id_type=pl.DeviceIdType.MESH,
+        )
+
+    def forward(stream, mask):
+        for bit in orders[stream]:
+            later = mask | bit
+            if later != mask and last_bit(stream, later) == bit:
+                block(stream, later).start()
+
+    for place in range(len(bits) + 1):
+        for stream in range(2):
+            block(stream, orders[stream][place]).start()
+
+    load.wait()
+
+    @pl.loop(0, points, unroll=2)
+    def _(point):
+        rows = coupled_ref[point].reshape(qpoints * branches * orbitals, lanes)
+        product = right_product(rows, right_weights(own_ref[point]))
+        for q in range(qpoints):
+            first = product[2 * q * orbitals : (2 * q + 1) * orbitals]
+            second = product[(2 * q + 1) * orbitals : (2 * q + 2) * orbitals]
+            high, low = split(jnp.concatenate([first, second], 1))
+            right_ref[point, q, :orbitals] = high
+            right_ref[point, q, orbitals:] = low
+
+    masks = sorted(range(1, ka_count), key=lambda mask: (mask.bit_count(), mask & 1, mask))
+    for mask in masks:
+        for stream in range(2):
+            block(stream, mask).wait_recv()
+            forward(stream, mask)
+    for mask in masks:
+        for stream in range(2):
+            block(stream, mask).wait_send()
 
     def piece(q, offset):
         target = lax.rem(me + offset, ka_count)
@@ -194,8 +256,7 @@
             @pl.loop(0, points, unroll=min(UNROLL, points))
             def _(point):
                 turned = left_weights(gauge_ref[index_ref[q * points + point]])
-                block = right_ref[point, q]
-                parts = left_product(turned, block[:orbitals], block[orbitals:])
+                parts = left_product(turned, right_ref[point, q, :orbitals], right_ref[point, q, orbitals:])
                 for branch in range(2):
                     held_ref[branch, :, point, :] = parts[branch]
 
@@ -348,13 +409,14 @@
     fine_rows = eig_right.shape[0]
     fine_rows_padded = -(-fine_rows // 8) * 8
     partial_size = fine_total * branches * orbitals * lanes * 4 * qpoints
-    if chunks == 1 and ka_count > 1 and pb_count > 1 and partial_size <= 8 * 1024 * 1024:
+    power = ka_count & (ka_count - 1) == 0 and points % 2 == 0
+    if chunks == 1 and power and ka_count > 1 and pb_count > 1 and partial_size <= 8 * 1024 * 1024:
         ka_others, pb_others = ka_count - 1, pb_count - 1
         vmem = pl.BlockSpec(memory_space=pltpu.VMEM)
         smem = pl.BlockSpec(memory_space=pltpu.SMEM)
         summed = pl.pallas_call(
             window_kernel,
-            in_specs=[smem, smem] + [vmem] * 8,
+            in_specs=[smem, smem, vmem, pl.BlockSpec(memory_space=pl.ANY)] + [vmem] * 6,
             out_specs=vmem,
             out_shape=jax.ShapeDtypeStruct((fine_rows, lanes), jnp.float32),
             scratch_shapes=[
@@ -368,13 +430,19 @@
                 pltpu.SemaphoreType.DMA((qpoints, ka_others)),
                 pltpu.SemaphoreType.DMA((pb_others,)),
                 pltpu.SemaphoreType.DMA((pb_others,)),
+                pltpu.VMEM((ka_count * points, orbitals, lanes), jnp.float32),
+                pltpu.VMEM(coupling.shape, jnp.float32),
+                pltpu.VMEM((points, qpoints, 2 * orbitals, 2 * lanes), jnp.bfloat16),
+                pltpu.SemaphoreType.DMA((2, ka_others)),
+                pltpu.SemaphoreType.DMA((2, ka_others)),
+                pltpu.SemaphoreType.DMA,
             ],
             compiler_params=pltpu.CompilerParams(
                 vmem_limit_bytes=VMEM_LIMIT, collective_id=0, has_side_effects=True
             ),
             name="window",
         )(
-            own_rows.reshape(-1), scalars, all_gauge, right, table[0], eig_right, eig_left,
+            own_rows.reshape(-1), scalars, gauge, coupling, table[0], eig_right, eig_left,
             energy_lanes, gap_lanes, filled_lanes,
         )
         return summed[:, :orbitals]

time: 140 us -> 112 us (0.80)
  waiting for transfers between devices: 43.1 us -> 0 us
  Pallas kernels: 76.6 us -> 102 us
  between operations: 13.5 us -> 0.1 us
  local copies, waits for them, and re-layouts: 3.79 us -> 6.25 us
    all_gather x1 -> x0, waiting for transfers between devices: 42.4 us -> none  [shards(): all_gauge = lax.all_gather(gauge, 'ka', axis=0, tiled=True)]
    pallas_call x2 -> x1, Pallas kernels: 76.6 us -> 102 us  [shards(): pl.pallas_call(window_kernel, in_specs=[smem, smem, vmem, pl.BlockSpec(me...]
    unnamed x12 -> x10, local copies, waits for them, and re-layouts: 2.57 us -> 4.34 us
  transfers between devices with their start and end apart: 1 -> 0, of which waited for: 1 -> 0; matrix products, arithmetic and copies ran while one was open for 3% -> 0% of each run, Pallas kernels for 8% -> 0%
where the time goes in v3:
time: 112 us; the launch traced here: 111 us
  Pallas kernels  102 us (91%)
  local copies, waits for them, and re-layouts  6.25 us (6%)
  other arithmetic  2.66 us (2%)
    pallas_call x1, Pallas kernels, shards(): pl.pallas_call(window_kernel, in_specs=[smem, smem, vmem, pl.BlockSpec(me...  102 us
    unnamed x10, local copies, waits for them, and re-layouts  4.34 us

profile of v3, /device:TPU:0, one launch (start us, length us, event | category | flops | bytes accessed | tf_op | source)
XLA Modules:
  0.0 111.4 jit_solution(2474973715509180982)
XLA Ops:
  0.0 0.0 copy-start
  0.1 0.8 pad_maximum_fusion.2.energy_ref
  0.9 0.0 copy-done
  0.9 0.1 reshape.316.index_ref
  1.0 0.8 slice_bitcast_fusion.1
  1.8 0.8 copy.13
  2.5 0.1 stack_reshape.3
  2.7 0.7 convert_element_type.15
  3.4 0.1 broadcast_subtract_fusion.1
  3.4 0.1 broadcast_subtract_fusion.2
  3.5 0.1 broadcast_subtract_fusion
  3.6 0.2 cosine_reduce_fusion.2
  3.8 0.6 cosine_reduce_fusion.1
  4.5 0.1 broadcast_in_dim.5.filled_ref
  4.6 0.8 broadcast_in_dim.4.gap_ref
  5.4 0.0 copy-start.1
  5.4 1.2 %copy-done.1 = f32[32,64,128]{2,1,0:T(8,128)S(1)} copy-done((f32[32,64,128]{2,1,0:T(8,128)S(1)}, f32[32,64,128]{2,1,0:T(8,128)}, u32[]{:S(2)}) %copy-start.1) | copy-done | bytes 1048600
  6.6 0.0 copy-start.2
  6.6 0.9 copy-done.2
  7.6 0.0 copy-start.3
  7.6 0.8 copy-done.3
  8.4 102.4 %window.1 = f32[2,128]{1,0:T(2,128)S(1)} custom-call(s32[128]{0:T(128)S(1)} %reshape.316.index_ref, f32[3,8]{1,0:T(4,128)S(1)} %pad_maximum_fusion.1.scalars_ref, f32[32,64,128]{2,1,0:T(8,128)S(1)} %copy-done.1, f32[32,4,2,64,128]{4,3,2,1,0:T(8,128)} %coupling_ref.1, f32[32,32]{1,0:T(8,128)S(1)} %bitcast.12, f32[2,64,128]{2,1,0:T(8,128)S(1)} %copy-done.3, ...), custom_call_target="tpu_custom_call" | custom-call | tf_op jit(solution)/shard_map/window/pallas_call | solution.py:417
  110.8 0.6 copy.15
  (10 shorter events, 0.1 us)
Async XLA Ops:
  0.0 0.9 copy-start
  5.4 1.2 %copy-start.1 = (f32[32,64,128]{2,1,0:T(8,128)S(1)}, f32[32,64,128]{2,1,0:T(8,128)}, u32[]{:S(2)}) copy-start(f32[32,64,128]{2,1,0:T(8,128)} %own_ref.1) | copy-start | bytes 3145732
  6.6 0.9 copy-start.2
  7.6 0.8 copy-start.3

commit v4 on v3

--- a/solution.py
+++ b/solution.py
@@ -15,7 +15,7 @@
 NK = 256
 BROADEN = 0.1
 THERMAL = 0.05
-VMEM_LIMIT = 48 * 1024 * 1024
+VMEM_LIMIT = 56 * 1024 * 1024
 UNROLL = 4
 
 
@@ -146,7 +146,7 @@
     energy_ref, gap_ref, filled_ref, out_ref,
     held_ref, partial_ref, arrived_ref, total_ref, terms_ref, others_ref,
     send_sem, recv_sem, terms_send, terms_recv,
-    gauge_ref, coupled_ref, right_ref, gather_send, gather_recv, load_sem,
+    gauge_ref, coupled_ref, right_ref, gather_send, gather_recv, load_sem, turned_ref,
 ):
     load = pltpu.make_async_copy(coupling_ref, coupled_ref, load_sem)
     load.start()
@@ -224,12 +224,32 @@
             right_ref[point, q, :orbitals] = high
             right_ref[point, q, orbitals:] = low
 
-    masks = sorted(range(1, ka_count), key=lambda mask: (mask.bit_count(), mask & 1, mask))
-    for mask in masks:
-        for stream in range(2):
-            block(stream, mask).wait_recv()
-            forward(stream, mask)
-    for mask in masks:
+    def turn(mask):
+        start = flipped(mask) * points
+
+        @pl.loop(0, points, unroll=min(UNROLL, points))
+        def _(point):
+            high, low = split(gauge_ref[start + point])
+            turned_ref[start + point] = jnp.concatenate([high, low], 0).T
+
+    def arrive(masks):
+        for mask in masks:
+            for stream in range(2):
+                block(stream, mask).wait_recv()
+                forward(stream, mask)
+
+    turn(0)
+    arrive([1])
+    turn(1)
+    for count in range(1, len(bits) + 1):
+        group = [mask for mask in range(2, ka_count, 2) if mask.bit_count() == count]
+        arrive(group)
+        for mask in group:
+            turn(mask)
+        for mask in group:
+            arrive([mask + 1])
+            turn(mask + 1)
+    for mask in range(1, ka_count):
         for stream in range(2):
             block(stream, mask).wait_send()
 
@@ -255,7 +275,8 @@
         def _():
             @pl.loop(0, points, unroll=min(UNROLL, points))
             def _(point):
-                turned = left_weights(gauge_ref[index_ref[q * points + point]])
+                turned = turned_ref[index_ref[q * points + point]]
+                turned = jnp.concatenate([turned, turned], 1)
                 parts = left_product(turned, right_ref[point, q, :orbitals], right_ref[point, q, orbitals:])
                 for branch in range(2):
                     held_ref[branch, :, point, :] = parts[branch]
@@ -436,6 +457,7 @@
                 pltpu.SemaphoreType.DMA((2, ka_others)),
                 pltpu.SemaphoreType.DMA((2, ka_others)),
                 pltpu.SemaphoreType.DMA,
+                pltpu.VMEM((ka_count * points, 2 * orbitals, lanes), jnp.bfloat16),
             ],
             compiler_params=pltpu.CompilerParams(
                 vmem_limit_bytes=VMEM_LIMIT, collective_id=0, has_side_effects=True

time: 112 us -> 114 us (1.018)
  Pallas kernels: 102 us -> 104 us
  other arithmetic: 2.66 us -> 4.4 us
    unnamed x10 -> x4, local copies, waits for them, and re-layouts: 4.34 us -> 2 us
    pallas_call x1, Pallas kernels: 102 us -> 104 us  [shards(): pl.pallas_call(window_kernel, in_specs=[smem, smem, vmem, pl.BlockSpec(me...]
where the time goes in v4:
time: 114 us
  Pallas kernels  104 us (91%)
  local copies, waits for them, and re-layouts  5.86 us (5%)
  other arithmetic  4.4 us (4%)
    pallas_call x1, Pallas kernels, shards(): pl.pallas_call(window_kernel, in_specs=[smem, smem, vmem, pl.BlockSpec(me...  104 us

profile of v4, /device:TPU:0, one launch (start us, length us, event | category | flops | bytes accessed | tf_op | source)
XLA Modules:
  0.0 114.1 jit_solution(2237837556492481120)
XLA Ops:
  0.0 0.0 copy-start
  0.1 1.4 %pad_maximum_fusion.2.energy_ref = f32[2,128]{1,0:T(2,128)} fusion(f32[2,64]{1,0:T(2,128)} %param.16), kind=kLoop, calls=%fused_computation.45 | loop fusion | flops 256 | bytes 1536 | tf_op jit(solution)/shard_map/concatenate | solution.py:425
  1.4 0.0 copy-done
  1.5 0.6 reshape.316.index_ref
  2.1 0.8 slice_bitcast_fusion.1
  2.9 0.8 copy.13
  3.6 0.1 stack_reshape.3
  3.7 0.6 pad_maximum_fusion.1.scalars_ref
  4.3 0.7 convert_element_type.15
  5.0 0.1 broadcast_subtract_fusion.1
  5.1 0.1 broadcast_subtract_fusion.2
  5.2 0.1 broadcast_subtract_fusion
  5.3 0.2 cosine_reduce_fusion.2
  5.5 0.6 cosine_reduce_fusion.1
  6.1 0.6 pad_maximum_fusion
  6.7 0.8 broadcast_in_dim.5.filled_ref
  7.6 1.5 %broadcast_in_dim.4.gap_ref = f32[2,4,64,128]{3,2,1,0:T(8,128)} broadcast(f32[2,4,64]{2,1,0:T(4,128)} %param.17), dimensions={0,1,2} | broadcast | bytes 264192 | tf_op jit(solution)/shard_map/broadcast_in_dim | solution.py:426
  9.1 103.7 %window.1 = f32[2,128]{1,0:T(2,128)} custom-call(s32[128]{0:T(128)} %reshape.316.index_ref, f32[3,8]{1,0:T(4,128)} %pad_maximum_fusion.1.scalars_ref, f32[32,64,128]{2,1,0:T(8,128)} %own_ref.1, f32[32,4,2,64,128]{4,3,2,1,0:T(8,128)} %coupling_ref.1, f32[32,32]{1,0:T(8,128)} %bitcast.12, f32[2,64,128]{2,1,0:T(8,128)} %fine_right_ref.1, ...), custom_call_target="tpu_custom_call" | custom-call | tf_op jit(solution)/shard_map/window/pallas_call | solution.py:438
  112.8 1.2 %copy.15 = f32[2,64]{1,0:T(2,128)} copy(f32[2,64]{1,0:T(2,128)} %bitcast.13) | data formatting | bytes 1024
  (8 shorter events, 0.1 us)
Async XLA Ops:
  0.0 1.5 %copy-start = (s32[16,32]{1,0:T(8,128)S(1)}, s32[16,32]{1,0:T(8,128)}, u32[]{:S(2)}) copy-start(s32[16,32]{1,0:T(8,128)} %param.12) | copy-start | bytes 6148

commit v5 on v3

--- a/solution.py
+++ b/solution.py
@@ -146,7 +146,7 @@
     energy_ref, gap_ref, filled_ref, out_ref,
     held_ref, partial_ref, arrived_ref, total_ref, terms_ref, others_ref,
     send_sem, recv_sem, terms_send, terms_recv,
-    gauge_ref, coupled_ref, right_ref, gather_send, gather_recv, load_sem,
+    gauge_ref, coupled_ref, right_ref, gather_send, gather_recv, load_sem, handed_ref, handed_send, handed_recv,
 ):
     load = pltpu.make_async_copy(coupling_ref, coupled_ref, load_sem)
     load.start()
@@ -233,13 +233,29 @@
         for stream in range(2):
             block(stream, mask).wait_send()
 
-    def piece(q, offset):
-        target = lax.rem(me + offset, ka_count)
+    sibling = me + 1 - 2 * lax.rem(me, 2)
+    pairs = ka_count // 2
+
+    def owned(device, step):
+        return lax.rem(device + 2 * step, ka_count)
+
+    def handed(q, step):
+        return pltpu.make_async_remote_copy(
+            src_ref=partial_ref.at[q, pl.ds(owned(sibling, step) * fine, fine)],
+            dst_ref=handed_ref.at[q, step],
+            send_sem=handed_send.at[q, step],
+            recv_sem=handed_recv.at[q, step],
+            device_id=(sibling, layer),
+            device_id_type=pl.DeviceIdType.MESH,
+        )
+
+    def piece(q, step):
+        target = owned(me, step)
         return pltpu.make_async_remote_copy(
             src_ref=partial_ref.at[q, pl.ds(target * fine, fine)],
-            dst_ref=arrived_ref.at[q, offset - 1],
-            send_sem=send_sem.at[q, offset - 1],
-            recv_sem=recv_sem.at[q, offset - 1],
+            dst_ref=arrived_ref.at[q, step - 1],
+            send_sem=send_sem.at[q, step - 1],
+            recv_sem=recv_sem.at[q, step - 1],
             device_id=(target, layer),
             device_id_type=pl.DeviceIdType.MESH,
         )
@@ -249,7 +265,7 @@
     if padded != points:
         held_ref[...] = jnp.zeros_like(held_ref)
 
-    @pl.loop(0, qpoints + 1)
+    @pl.loop(0, qpoints + 2)
     def _(q):
         @pl.when(q < qpoints)
         def _():
@@ -273,18 +289,29 @@
                         part[fine_total:], -1.0
                     )
 
-            for offset in range(1, ka_count):
-                piece(q, offset).start()
-
-        @pl.when(q > 0)
+            for step in range(pairs):
+                handed(q, step).start()
+
+        @pl.when((q > 0) & (q < qpoints + 1))
         def _():
-            done = q - 1
-            for offset in range(1, ka_count):
-                piece(done, offset).wait()
+            last = q - 1
+            for step in range(pairs):
+                handed(last, step).wait()
+            for step in list(range(1, pairs)) + [0]:
+                rows = pl.ds(owned(me, step) * fine, fine)
+                partial_ref[last, rows] = partial_ref[last, rows] + handed_ref[last, step]
+                if step > 0:
+                    piece(last, step).start()
+
+        @pl.when(q > 1)
+        def _():
+            done = q - 2
+            for step in range(1, pairs):
+                piece(done, step).wait()
             for f in range(fine):
                 rows = partial_ref[done, me * fine + f]
-                for offset in range(1, ka_count):
-                    rows = rows + arrived_ref[done, offset - 1, f]
+                for step in range(1, pairs):
+                    rows = rows + arrived_ref[done, step - 1, f]
                 product = right_product(
                     rows.reshape(branches * orbitals, lanes), right_weights(fine_right_ref[f])
                 )
@@ -410,7 +437,7 @@
     fine_rows_padded = -(-fine_rows // 8) * 8
     partial_size = fine_total * branches * orbitals * lanes * 4 * qpoints
     power = ka_count & (ka_count - 1) == 0 and points % 2 == 0
-    if chunks == 1 and power and ka_count > 1 and pb_count > 1 and partial_size <= 8 * 1024 * 1024:
+    if chunks == 1 and power and ka_count > 2 and pb_count > 1 and partial_size <= 8 * 1024 * 1024:
         ka_others, pb_others = ka_count - 1, pb_count - 1
         vmem = pl.BlockSpec(memory_space=pltpu.VMEM)
         smem = pl.BlockSpec(memory_space=pltpu.SMEM)
@@ -436,6 +463,9 @@
                 pltpu.SemaphoreType.DMA((2, ka_others)),
                 pltpu.SemaphoreType.DMA((2, ka_others)),
                 pltpu.SemaphoreType.DMA,
+                pltpu.VMEM((qpoints, ka_count // 2, fine_rows, branches, orbitals, lanes), jnp.float32),
+                pltpu.SemaphoreType.DMA((qpoints, ka_count // 2)),
+                pltpu.SemaphoreType.DMA((qpoints, ka_count // 2)),
             ],
             compiler_params=pltpu.CompilerParams(
                 vmem_limit_bytes=VMEM_LIMIT, collective_id=0, has_side_effects=True

time: 112 us -> 101 us (0.902)
  Pallas kernels: 102 us -> 91.6 us
    pallas_call x1, Pallas kernels: 102 us -> 91.6 us  [shards(): pl.pallas_call(window_kernel, in_specs=[smem, smem, vmem, pl.BlockSpec(me...]
where the time goes in v5:
time: 101 us
  Pallas kernels  91.6 us (91%)
  local copies, waits for them, and re-layouts  6.25 us (6%)
  other arithmetic  2.66 us (3%)
    pallas_call x1, Pallas kernels, shards(): pl.pallas_call(window_kernel, in_specs=[smem, smem, vmem, pl.BlockSpec(me...  91.6 us
    unnamed x10, local copies, waits for them, and re-layouts  4.34 us

profile of v5, /device:TPU:0, one launch (start us, length us, event | category | flops | bytes accessed | tf_op | source)
XLA Modules:
  0.0 100.6 jit_solution(1434631729248167908)
XLA Ops:
  0.0 0.0 copy-start
  0.1 0.8 pad_maximum_fusion.2.energy_ref
  0.9 0.0 copy-done
  0.9 0.1 reshape.316.index_ref
  1.0 0.8 slice_bitcast_fusion.1
  1.8 0.8 copy.13
  2.5 0.1 stack_reshape.3
  2.7 0.7 convert_element_type.15
  3.4 0.1 broadcast_subtract_fusion.1
  3.4 0.1 broadcast_subtract_fusion.2
  3.5 0.1 broadcast_subtract_fusion
  3.6 0.2 cosine_reduce_fusion.2
  3.8 0.6 cosine_reduce_fusion.1
  4.5 0.1 broadcast_in_dim.5.filled_ref
  4.6 0.8 broadcast_in_dim.4.gap_ref
  5.4 0.0 copy-start.1
  5.4 1.2 %copy-done.1 = f32[32,64,128]{2,1,0:T(8,128)S(1)} copy-done((f32[32,64,128]{2,1,0:T(8,128)S(1)}, f32[32,64,128]{2,1,0:T(8,128)}, u32[]{:S(2)}) %copy-start.1) | copy-done | bytes 1048600
  6.6 0.0 copy-start.2
  6.6 0.9 copy-done.2
  7.6 0.0 copy-start.3
  7.6 0.8 copy-done.3
  8.4 91.6 %window.1 = f32[2,128]{1,0:T(2,128)S(1)} custom-call(s32[128]{0:T(128)S(1)} %reshape.316.index_ref, f32[3,8]{1,0:T(4,128)S(1)} %pad_maximum_fusion.1.scalars_ref, f32[32,64,128]{2,1,0:T(8,128)S(1)} %copy-done.1, f32[32,4,2,64,128]{4,3,2,1,0:T(8,128)} %coupling_ref.1, f32[32,32]{1,0:T(8,128)S(1)} %bitcast.12, f32[2,64,128]{2,1,0:T(8,128)S(1)} %copy-done.3, ...), custom_call_target="tpu_custom_call" | custom-call | tf_op jit(solution)/shard_map/window/pallas_call | solution.py:444
  100.0 0.6 copy.15
  (10 shorter events, 0.1 us)
Async XLA Ops:
  0.0 0.9 copy-start
  5.4 1.2 %copy-start.1 = (f32[32,64,128]{2,1,0:T(8,128)S(1)}, f32[32,64,128]{2,1,0:T(8,128)}, u32[]{:S(2)}) copy-start(f32[32,64,128]{2,1,0:T(8,128)} %own_ref.1) | copy-start | bytes 3145732
  6.6 0.9 copy-start.2
  7.6 0.8 copy-start.3
